TPU v7x, 32 devices: a whole 2x2x4 slice. The times are simulated.
32 devices in a mesh: dp: 8 (over y, x, core), expert: 4 (over z).
Axes of the slice: x: 2, y: 2, z: 4, core: 2. Of those that a mesh axis runs over, the one named last changes fastest.
Arguments:
- tokens: bfloat16 [1024, 6144], P('dp'), may hold values from -6 to 6
- routes: int32 [1024, 2], P('dp'), may hold values from 0 to 3, all different within a row; in each aligned block of 128 rows (0 to 127, 128 to 255, ...) at most 128 rows name the same one
- gates: float32 [1024, 2], P('dp'), may hold values from 0.1 to 1
- capacity: int32 [4], replicated, may hold values from 64 to 128, as said below
- w_gate: bfloat16 [4, 6144, 8192], P('expert', None, 'dp'), may hold values from -0.078125 to 0.078125
- w_up: bfloat16 [4, 6144, 8192], P('expert', None, 'dp'), may hold values from -0.078125 to 0.078125
- w_down: bfloat16 [4, 8192, 6144], P('expert', 'dp'), may hold values from -0.0625 to 0.0625
Outputs:
- mixed: bfloat16 [1024, 6144], P('dp', 'expert')
Inputs may be any that keep to these rules, and one draw needn't show every extreme that they name: `routes`: each token names two different experts. Within the 128 tokens of one index of dp no expert is named by more than 128 tokens, and in some shards one expert is named by exactly 128. Some expert's capacity is exactly 128.
All inputs are finite; a program needn't handle non-finite values.
Results may differ from a plain program's by a relative error of at most 0.015.
Values may be sent and summed in bfloat16 or wider, within the bound.
A program may use at most 128 MiB of HBM per device.

v0:
```python
import jax
import jax.numpy as jnp
from jax import lax
from jax.sharding import PartitionSpec as P


def on_device(tokens, routes, gates, capacity, w_gate, w_up, w_down):
    owner_index = lax.axis_index("expert")
    group_size = lax.axis_size("expert")
    local_rows = tokens.shape[0]
    num_experts = group_size * w_gate.shape[0]
    slot_count = 4 * local_rows // num_experts
    matched = routes == owner_index
    member = jnp.any(matched, axis=-1).astype(jnp.int32)
    weight = jnp.sum(jnp.where(matched, gates, 0.0), axis=-1)
    position = jnp.cumsum(member) - member
    limit_value = jnp.sum(
        jnp.where(jnp.arange(num_experts, dtype=jnp.int32) == owner_index, capacity, 0)
    )
    retained = (member == 1) & (position < limit_value)
    slot_ids = jnp.arange(slot_count, dtype=jnp.int32)
    selector = (retained[None, :] & (position[None, :] == slot_ids[:, None])).astype(jnp.bfloat16)
    slot_rows = jnp.dot(selector, tokens, preferred_element_type=jnp.float32).astype(jnp.bfloat16)
    gate_panel = w_gate[0]
    up_panel = w_up[0]
    down_panel = w_down[0]
    block_rows = lax.all_gather(slot_rows, "dp", axis=0, tiled=True)
    gate_value = jnp.dot(block_rows, gate_panel, preferred_element_type=jnp.float32)
    up_value = jnp.dot(block_rows, up_panel, preferred_element_type=jnp.float32)
    hidden = (jax.nn.silu(gate_value) * up_value).astype(jnp.bfloat16)
    partial_value = jnp.dot(hidden, down_panel, preferred_element_type=jnp.float32)
    returned = lax.psum_scatter(
        partial_value.astype(jnp.bfloat16), "dp", scatter_dimension=0, tiled=True
    ).astype(jnp.float32)
    placed = jnp.einsum(
        "ct,cd->td", selector.astype(jnp.float32), returned, precision=lax.Precision.HIGHEST
    )
    weighted = weight[:, None] * placed
    result = lax.psum_scatter(
        weighted.astype(jnp.bfloat16), "expert", scatter_dimension=1, tiled=True
    )
    return result


def solution(mesh):
    in_specs = (
        P("dp", None),
        P("dp", None),
        P("dp", None),
        P(),
        P("expert", None, "dp"),
        P("expert", None, "dp"),
        P("expert", "dp", None),
    )
    out_specs = P("dp", "expert")
    return jax.shard_map(
        on_device, mesh=mesh, in_specs=in_specs, out_specs=out_specs, check_vma=False
    )
```

profile of v0, /device:TPU:0, one launch (start us, length us, event | category | flops | bytes accessed | tf_op | source)
XLA Modules:
  0.0 277.2 jit_solution(16676860792243399009)
XLA Ops:
  6.5 0.0 copy-start
  6.5 0.0 all-gather.2.cloned.1.call-start
  6.5 1.4 fusion.19
  8.0 0.7 fusion.20
  8.7 0.1 copy.9
  8.8 0.2 reduce-window.7
  8.9 0.1 reduce
  9.1 0.7 compare_and_fusion
  9.7 0.0 copy-done
  9.7 1.8 convolution_convert_fusion
  11.5 0.0 all-gather.2.cloned.1.call-update
  11.5 0.0 reduce-scatter.3.cloned.1.call-start
  11.6 74.9 %all-gather.2.cloned.1.call-done = bf16[1024,6144]{1,0:T(8,128)(2,1)} async-done(((bf16[128,6144]{1,0:T(8,128)(2,1)}), bf16[1024,6144]{1,0:T(8,128)(2,1)}) %all-gather.2.cloned.1.call-update) | async-done | bytes 12582928 | tf_op jit(solution)/shard_map/all_gather | solution.py:27
  86.5 0.0 copy-start.4
  86.5 17.2 %fusion.2 = f32[1024,1024]{1,0:T(8,128)S(1)} fusion(bf16[1024,6144]{1,0:T(8,128)(2,1)} %all-gather.2.cloned.1.call-done, bf16[1,6144,1024]{2,1,0:T(8,128)(2,1)} %param.12), kind=kOutput, calls=%fused_computation.2 | convolution fusion | flops 12884901888 | bytes 29360128 | tf_op jit(solution)/shard_map/dot_general | solution.py:29
  103.8 0.0 copy-done.4
  103.8 15.8 %multiply_convert_fusion = bf16[1024,1024]{1,0:T(8,128)(2,1)S(1)} fusion(f32[1024,1024]{1,0:T(8,128)S(1)} %fusion.2, bf16[1024,6144]{1,0:T(8,128)(2,1)S(1)} %copy-done.4, bf16[1,6144,1024]{2,1,0:T(8,128)(2,1)} %param.11), kind=kOutput, calls=%fused_computation.10 | convolution fusion | flops 12891193344 | bytes 31457280 | tf_op jit(solution)/shard_map/dot_general | solution.py:28
  119.5 19.9 %fusion.6 = bf16[1024,6144]{1,0:T(8,128)(2,1)} fusion(bf16[1024,1024]{1,0:T(8,128)(2,1)S(1)} %multiply_convert_fusion, bf16[1,1024,6144]{2,1,0:T(8,128)(2,1)} %param.13), kind=kOutput, calls=%fused_computation.6 | convolution fusion | flops 12891193344 | bytes 27262976 | tf_op jit(solution)/shard_map/dot_general | solution.py:31
  139.5 0.0 copy-start.2
  139.5 0.0 copy-start.3
  139.5 0.0 reduce-scatter.3.cloned.1.call-update
  139.5 0.0 copy-start.1
  139.5 0.0 reduce-scatter.5.cloned.1.call-start
  139.6 0.6 copy-done.2
  140.2 0.0 copy-done.3
  140.2 91.9 %reduce-scatter.3.cloned.1.call-done = bf16[128,6144]{1,0:T(8,128)(2,1)} async-done(((bf16[1024,6144]{1,0:T(8,128)(2,1)}), bf16[128,6144]{1,0:T(8,128)(2,1)}) %reduce-scatter.3.cloned.1.call-update) | async-done | bytes 1572880 | tf_op jit(solution)/shard_map/reduce_scatter | solution.py:32
  232.1 3.2 %fusion.9 = bf16[128,6144]{1,0:T(8,128)(2,1)} fusion(bf16[128,6144]{1,0:T(8,128)(2,1)} %reduce-scatter.3.cloned.1.call-done, f32[128]{0:T(128)S(1)} %select_reduce_fusion, s32[128]{0:T(128)S(1)} %convert_subtract_fusion, pred[128]{0:T(512)(128)(4,1)S(1)} %compare_and_fusion), kind=kOutput, calls=%fused_computation.8 | convolution fusion | flops 202932224 | bytes 3146880 | tf_op jit(solution)/shard_map/ct,cd->td/dot_general | solution.py:35
  235.2 0.0 reduce-scatter.5.cloned.1.call-update
  235.3 35.4 %reduce-scatter.5.cloned.1.call-done = bf16[128,1536]{1,0:T(8,128)(2,1)} async-done(((bf16[128,6144]{1,0:T(8,128)(2,1)}), bf16[128,1536]{1,0:T(8,128)(2,1)}) %reduce-scatter.5.cloned.1.call-update) | async-done | bytes 393232 | tf_op jit(solution)/shard_map/reduce_scatter | solution.py:39
  270.7 0.0 copy-done.1
  (3 shorter events, 0.0 us)
Async XLA Ops:
  6.5 3.2 %copy-start = (bf16[128,6144]{1,0:T(8,128)(2,1)S(1)}, bf16[128,6144]{1,0:T(8,128)(2,1)}, u32[]{:S(2)}) copy-start(bf16[128,6144]{1,0:T(8,128)(2,1)} %param.7) | copy-start | bytes 4718596
  6.5 80.0 %all-gather.2.cloned.1.call-start = ((), (), s32[]{:S(2)}) async-start(), calls=%async_computation.2 | async-start | bytes 14155776 | tf_op jit(solution)/shard_map/all_gather | solution.py:27
  11.5 220.5 %reduce-scatter.3.cloned.1.call-start = ((), (), s32[]{:S(2)}) async-start(), calls=%async_computation.3 | async-start | bytes 14155776 | tf_op jit(solution)/shard_map/reduce_scatter | solution.py:32
  86.5 17.3 %copy-start.4 = (bf16[1024,6144]{1,0:T(8,128)(2,1)S(1)}, bf16[1024,6144]{1,0:T(8,128)(2,1)}, u32[]{:S(2)}) copy-start(bf16[1024,6144]{1,0:T(8,128)(2,1)} %all-gather.2.cloned.1.call-done) | copy-start | bytes 37748740
  139.5 0.7 copy-start.2
  139.5 0.7 copy-start.3
  139.5 131.2 %copy-start.1 = (bf16[128,6144]{1,0:T(8,128)(2,1)S(1)}, bf16[128,6144]{1,0:T(8,128)(2,1)}, u32[]{:S(2)}) copy-start(bf16[128,6144]{1,0:T(8,128)(2,1)} %param.7) | copy-start | bytes 4718596
  139.5 131.2 %reduce-scatter.5.cloned.1.call-start = ((), (), s32[]{:S(2)}) async-start(), calls=%async_computation.4 | async-start | bytes 1966080 | tf_op jit(solution)/shard_map/reduce_scatter | solution.py:39
Sparse Core Ops, SparseCore 0:
  11.6 74.8 all-gather.1
  139.6 92.3 reduce-scatter.2
  235.4 35.2 reduce-scatter.4
where the time goes:
time: 277 us
  waiting for transfers between devices  202 us (73%)
  matrix products  57.9 us (21%)
  between operations  13.2 us (5%)
  other arithmetic  3.07 us (1%)
    reduce_scatter x1, waiting for transfers between devices, on_device(): lax.psum_scatter(partial_value.astype(jnp.bfloat16), 'dp', scatter_dimens...  91.9 us
    all_gather x1, waiting for transfers between devices, on_device(): block_rows = lax.all_gather(slot_rows, 'dp', axis=0, tiled=True)  74.9 us
    reduce_scatter x1, waiting for transfers between devices, on_device(): lax.psum_scatter(weighted.astype(jnp.bfloat16), 'expert', scatter_dimensi...  35.4 us
    dot_general x1, matrix products, on_device(): jnp.dot(hidden, down_panel, preferred_element_type=jnp.float32)  19.9 us
    dot_general x1, matrix products, on_device(): up_value = jnp.dot(block_rows, up_panel, preferred_element_type=jnp.float32)  17.2 us
    dot_general x1, matrix products, on_device(): jnp.dot(block_rows, gate_panel, preferred_element_type=jnp.float32)  15.8 us
  transfers between devices with their start and end apart: 3, of which 3 were waited for; matrix products, arithmetic and copies ran while one was open for 0% of the time, Pallas kernels for 0%

commit v1 on v0

v1 whole, which is shorter than its diff:
```python
import jax
import jax.numpy as jnp
from jax import lax
from jax.experimental import pallas as pl
from jax.experimental.pallas import tpu as pltpu
from jax.sharding import PartitionSpec as P

MESH = pl.DeviceIdType.MESH
CHIPS = 4
STEPS = 4


def keep_weight(routes, gates, capacity, owner, num_experts):
    matched = routes == owner
    member = jnp.any(matched, axis=-1).astype(jnp.int32)
    weight = jnp.sum(jnp.where(matched, gates, 0.0), axis=-1)
    rows = routes.shape[0]
    order = jnp.arange(rows, dtype=jnp.int32)
    before = order[None, :] < order[:, None]
    position = jnp.sum(jnp.where(before, member[None, :], 0), axis=-1)
    limit_value = jnp.sum(
        jnp.where(jnp.arange(num_experts, dtype=jnp.int32) == owner, capacity, 0)
    )
    retained = (member == 1) & (position < limit_value)
    return retained, position, weight


def fused(tok, wt, wg_hbm, wu_hbm, wd_hbm, out, x, wg, wu, wd, h, c, r, zr,
          load_sem, wd_sem, ag_send, ag_recv, fw_send, fw_recv, sib_send, sib_recv,
          rs_send, rs_recv, z_send, z_recv):
    rows, width = tok.shape
    quarter = width // STEPS
    hidden = wg.shape[1]
    half = rows // 2
    me = lax.axis_index("dp")
    z = lax.axis_index("expert")
    core = lax.rem(me, 2)
    cx = lax.rem(me // 2, 2)
    cy = me // 4
    sibling = (me - core + (1 - core), z)

    def chip(g):
        return ((lax.rem(cy + g // 2, 2) * 2 + lax.rem(cx + g % 2, 2)) * 2 + core, z)

    def peer(s):
        return (me, lax.rem(z + s + 1, STEPS))

    def cols(s):
        return pl.ds(pl.multiple_of(lax.rem(z + s + 1, STEPS) * quarter, quarter), quarter)

    def remote(src, dst, ssem, rsem, device):
        return pltpu.make_async_remote_copy(
            src_ref=src, dst_ref=dst, send_sem=ssem, recv_sem=rsem,
            device_id=device, device_id_type=MESH)

    mine, other = pl.ds(0, rows), pl.ds(rows, rows)

    own = pltpu.make_async_copy(tok, x.at[0, mine], load_sem.at[0])
    own.start()
    load_g = pltpu.make_async_copy(wg_hbm, wg, load_sem.at[1])
    load_u = pltpu.make_async_copy(wu_hbm, wu, load_sem.at[2])
    load_g.start()
    load_u.start()

    def wd_copy(s, slot):
        return pltpu.make_async_copy(wd_hbm.at[:, cols(s)], wd.at[slot], wd_sem.at[slot])

    barrier = pltpu.get_barrier_semaphore()
    partners = [sibling, chip(1), chip(2), chip(3), peer(0), peer(1), peer(2)]
    for p in partners:
        pl.semaphore_signal(barrier, inc=1, device_id=p, device_id_type=MESH)
    pl.semaphore_wait(barrier, len(partners))

    gather = [
        remote(tok, x.at[1, mine], ag_send.at[1], ag_recv.at[1], chip(1)),
        remote(tok, x.at[2, mine], ag_send.at[2], ag_recv.at[2], chip(2)),
        remote(tok, x.at[0, other], fw_send.at[0], fw_recv.at[0], sibling),
    ]
    for copy in gather:
        copy.start()
    wd_copy(0, 0).start()
    wd_copy(1, 1).start()

    def forward(g):
        return remote(x.at[g, mine], x.at[g, other], fw_send.at[g], fw_recv.at[g], sibling)

    def sib_copy(g, s):
        return remote(x.at[g, other, cols(s)], c.at[g, :, cols(s)],
                      sib_send.at[g, s], sib_recv.at[g, s], sibling)

    def rs_copy(g, s):
        return remote(x.at[g, mine, cols(s)], r.at[g - 1, :, cols(s)],
                      rs_send.at[g - 1, s], rs_recv.at[g - 1, s], chip(g))

    def gate_up(g):
        tile = 256

        def body(n, carry):
            where = pl.ds(pl.multiple_of(n * tile, tile), tile)
            a = jnp.dot(x[g], wg[:, where], preferred_element_type=jnp.float32)
            b = jnp.dot(x[g], wu[:, where], preferred_element_type=jnp.float32)
            h[:, where] = (a / (1.0 + jnp.exp(-a)) * b).astype(jnp.bfloat16)
            return carry

        lax.fori_loop(0, hidden // tile, body, 0)

    def chip_sum(g, s):
        sib_copy(g, s).wait_recv()
        if g > 0:
            tile = 16

            def body(i, carry):
                at = pl.ds(pl.multiple_of(i * tile, tile), tile)
                x[g, at, cols(s)] = (
                    x[g, at, cols(s)].astype(jnp.float32)
                    + c[g, at, cols(s)].astype(jnp.float32)).astype(jnp.bfloat16)
                return carry

            lax.fori_loop(0, rows // tile, body, 0)
            rs_copy(g, s).start()

    def down(g):
        tile = 256

        def step(s, carry):
            slot = lax.rem(s, 2)
            wd_copy(s, slot).wait()
            base = lax.rem(z + s + 1, STEPS) * quarter

            def body(n, inner):
                where = pl.ds(pl.multiple_of(n * tile, tile), tile)
                to = pl.ds(pl.multiple_of(base + n * tile, tile), tile)
                x[g, :, to] = jnp.dot(
                    h[...], wd[slot, :, where], preferred_element_type=jnp.float32
                ).astype(jnp.bfloat16)
                return inner

            lax.fori_loop(0, quarter // tile, body, 0)
            sib_copy(g, s).start()
            if g < CHIPS - 1:
                wd_copy(lax.rem(s + 2, STEPS), slot).start()
            else:
                @pl.when(s + 2 < STEPS)
                def _():
                    wd_copy(s + 2, slot).start()

            @pl.when(s > 0)
            def _():
                chip_sum(g, s - 1)

            return carry

        lax.fori_loop(0, STEPS, step, 0)
        chip_sum(g, STEPS - 1)

    own.wait()
    load_g.wait()
    load_u.wait()
    gather[2].wait()
    gate_up(0)
    down(0)

    gather[0].wait_recv()
    via_y = remote(x.at[1, pl.ds(0, half)], x.at[3, pl.ds(0, half)],
                   ag_send.at[3], ag_recv.at[3], chip(2))
    via_y.start()
    forward(1).start()
    gather[1].wait_recv()
    via_x = remote(x.at[2, pl.ds(half, half)], x.at[3, pl.ds(half, half)],
                   ag_send.at[0], ag_recv.at[0], chip(1))
    via_x.start()
    forward(2).start()
    forward(1).wait_recv()
    gate_up(1)
    via_y.wait_send()
    forward(1).wait_send()
    down(1)
    forward(2).wait_recv()
    gate_up(2)
    via_y.wait_recv()
    via_x.wait()
    forward(3).start()
    forward(2).wait_send()
    down(2)
    forward(3).wait()
    gate_up(3)
    down(3)

    def z_copy(s):
        return remote(x.at[0, mine, cols(s)], zr.at[s], z_send.at[s], z_recv.at[s], peer(s))

    tile = 16

    def total(s, at):
        value = x[0, at, cols(s)].astype(jnp.float32) + c[0, at, cols(s)].astype(jnp.float32)
        for g in range(1, CHIPS):
            value = value + r[g - 1, at, cols(s)].astype(jnp.float32)
        w = wt[at, 0:1]
        return jnp.where(w != 0.0, value * w, 0.0)

    def finish(s, carry):
        for g in range(1, CHIPS):
            rs_copy(g, s).wait_recv()

        def body(i, inner):
            at = pl.ds(pl.multiple_of(i * tile, tile), tile)
            x[0, at, cols(s)] = total(s, at).astype(jnp.bfloat16)
            return inner

        lax.fori_loop(0, rows // tile, body, 0)
        z_copy(s).start()
        return carry

    lax.fori_loop(0, STEPS - 1, finish, 0)
    last = STEPS - 1
    for g in range(1, CHIPS):
        rs_copy(g, last).wait_recv()
    for s in range(STEPS - 1):
        z_copy(s).wait_recv()

    def body(i, inner):
        at = pl.ds(pl.multiple_of(i * tile, tile), tile)
        value = total(last, at)
        for s in range(STEPS - 1):
            value = value + zr[s, at].astype(jnp.float32)
        out[at] = value.astype(jnp.bfloat16)
        return inner

    lax.fori_loop(0, rows // tile, body, 0)

    gather[0].wait_send()
    gather[1].wait_send()
    for s in range(STEPS):
        for g in range(CHIPS):
            sib_copy(g, s).wait_send()
            if g > 0:
                rs_copy(g, s).wait_send()
        if s < STEPS - 1:
            z_copy(s).wait_send()


def kernel_device(tokens, routes, gates, capacity, w_gate, w_up, w_down):
    rows, width = tokens.shape
    hidden = w_gate.shape[2]
    quarter = width // STEPS
    owner = lax.axis_index("expert")
    retained, _, weight = keep_weight(routes, gates, capacity, owner, capacity.shape[0])
    wt = jnp.broadcast_to(jnp.where(retained, weight, 0.0)[:, None], (rows, 128))
    any_space = pl.BlockSpec(memory_space=pl.ANY)
    vmem = pl.BlockSpec(memory_space=pltpu.VMEM)
    dma = pltpu.SemaphoreType.DMA
    return pl.pallas_call(
        fused,
        out_shape=jax.ShapeDtypeStruct((rows, quarter), jnp.bfloat16),
        in_specs=[any_space, vmem, any_space, any_space, any_space],
        out_specs=vmem,
        scratch_shapes=[
            pltpu.VMEM((CHIPS, 2 * rows, width), jnp.bfloat16),
            pltpu.VMEM((width, hidden), jnp.bfloat16),
            pltpu.VMEM((width, hidden), jnp.bfloat16),
            pltpu.VMEM((2, hidden, quarter), jnp.bfloat16),
            pltpu.VMEM((2 * rows, hidden), jnp.bfloat16),
            pltpu.VMEM((CHIPS, rows, width), jnp.bfloat16),
            pltpu.VMEM((CHIPS - 1, rows, width), jnp.bfloat16),
            pltpu.VMEM((STEPS - 1, rows, quarter), jnp.bfloat16),
            dma((3,)), dma((2,)),
            dma((CHIPS,)), dma((CHIPS,)), dma((CHIPS,)), dma((CHIPS,)),
            dma((CHIPS, STEPS)), dma((CHIPS, STEPS)),
            dma((CHIPS - 1, STEPS)), dma((CHIPS - 1, STEPS)),
            dma((STEPS - 1,)), dma((STEPS - 1,)),
        ],
        cost_estimate=pl.CostEstimate(
            flops=2 * 3 * 2 * CHIPS * rows * width * hidden,
            bytes_accessed=2 * (6 * hidden * width),
            transcendentals=2 * CHIPS * rows * hidden),
        compiler_params=pltpu.CompilerParams(
            collective_id=0, has_side_effects=True, vmem_limit_bytes=60 * 2**20),
    )(tokens, wt, w_gate[0], w_up[0], w_down[0])


def plain_device(tokens, routes, gates, capacity, w_gate, w_up, w_down):
    owner_index = lax.axis_index("expert")
    group_size = lax.axis_size("expert")
    local_rows = tokens.shape[0]
    num_experts = group_size * w_gate.shape[0]
    slot_count = 4 * local_rows // num_experts
    retained, position, weight = keep_weight(routes, gates, capacity, owner_index, num_experts)
    slot_ids = jnp.arange(slot_count, dtype=jnp.int32)
    selector = (retained[None, :] & (position[None, :] == slot_ids[:, None])).astype(jnp.bfloat16)
    slot_rows = jnp.dot(selector, tokens, preferred_element_type=jnp.float32).astype(jnp.bfloat16)
    block_rows = lax.all_gather(slot_rows, "dp", axis=0, tiled=True)
    gate_value = jnp.dot(block_rows, w_gate[0], preferred_element_type=jnp.float32)
    up_value = jnp.dot(block_rows, w_up[0], preferred_element_type=jnp.float32)
    hidden = (jax.nn.silu(gate_value) * up_value).astype(jnp.bfloat16)
    partial_value = jnp.dot(hidden, w_down[0], preferred_element_type=jnp.float32)
    returned = lax.psum_scatter(
        partial_value.astype(jnp.bfloat16), "dp", scatter_dimension=0, tiled=True
    ).astype(jnp.float32)
    placed = jnp.einsum(
        "ct,cd->td", selector.astype(jnp.float32), returned, precision=lax.Precision.HIGHEST
    )
    weighted = weight[:, None] * placed
    return lax.psum_scatter(
        weighted.astype(jnp.bfloat16), "expert", scatter_dimension=1, tiled=True
    )


def solution(mesh):
    in_specs = (
        P("dp", None),
        P("dp", None),
        P("dp", None),
        P(),
        P("expert", None, "dp"),
        P("expert", None, "dp"),
        P("expert", "dp", None),
    )
    fits = mesh.shape["dp"] == 2 * CHIPS and mesh.shape["expert"] == STEPS
    on_device = kernel_device if fits else plain_device
    return jax.shard_map(
        on_device, mesh=mesh, in_specs=in_specs, out_specs=P("dp", "expert"), check_vma=False
    )
```

time: 277 us -> 160 us (0.58)
  waiting for transfers between devices: 202 us -> 0 us
  Pallas kernels: 0 us -> 154 us
  matrix products: 57.9 us -> 0 us
  between operations: 13.2 us -> 0.02 us
    pallas_call x0 -> x1, Pallas kernels: none -> 154 us  [kernel_device(): pl.pallas_call(fused, out_shape=jax.ShapeDtypeStruct((rows, quarter), jnp...]
    reduce_scatter x2 -> x0, waiting for transfers between devices: 127 us -> none  [the longest x1 91.9 us: on_device(): lax.psum_scatter(partial_value.astype(jnp.bfloat16), 'dp', scatter_dimens...]
    all_gather x1 -> x0, waiting for transfers between devices: 74.9 us -> none  [on_device(): block_rows = lax.all_gather(slot_rows, 'dp', axis=0, tiled=True)]
    dot_general x5 -> x0, matrix products: 57.9 us -> none  [the longest x1 19.9 us: on_device(): jnp.dot(hidden, down_panel, preferred_element_type=jnp.float32)]
  transfers between devices with their start and end apart: 3 -> 0, of which waited for: 3 -> 0; matrix products, arithmetic and copies ran while one was open for 0% -> 0% of each run, Pallas kernels for 0% -> 0%
where the time goes in v1:
time: 160 us
  Pallas kernels  154 us (96%)
  other arithmetic  3.47 us (2%)
  local copies, waits for them, and re-layouts  2.48 us (2%)
    pallas_call x1, Pallas kernels, kernel_device(): pl.pallas_call(fused, out_shape=jax.ShapeDtypeStruct((rows, quarter), jnp...  154 us

profile of v1, /device:TPU:0, one launch (start us, length us, event | category | flops | bytes accessed | tf_op | source)
XLA Modules:
  0.0 160.0 jit_solution(14354589701722125600)
XLA Ops:
  0.0 1.3 fusion
  1.3 0.7 fusion.1
  2.0 0.7 select_reduce_fusion.1
  2.7 0.1 select_reduce_fusion
  2.8 0.7 and_select_fusion
  3.5 0.7 broadcast_in_dim.38.wt
  4.2 154.0 %shard_map.73 = bf16[128,1536]{1,0:T(8,128)(2,1)} custom-call(bf16[128,6144]{1,0:T(8,128)(2,1)} %tok.1, f32[128,128]{1,0:T(8,128)} %broadcast_in_dim.38.wt, bf16[6144,1024]{1,0:T(8,128)(2,1)} %bitcast.3, bf16[6144,1024]{1,0:T(8,128)(2,1)} %bitcast.4, bf16[1024,6144]{1,0:T(8,128)(2,1)} %bitcast.5), custom_call_target="tpu_custom_call" | custom-call | flops 38654705664 | bytes 75497472 | tf_op jit(solution)/shard_map/pallas_call | solution.py:252
  158.2 1.8 %copy.9 = bf16[128,1536]{1,0:T(8,128)(2,1)} copy(bf16[128,1536]{1,0:T(8,128)(2,1)} %shard_map.73) | data formatting | bytes 786432
  (1 shorter events, 0.0 us)
